TPU v7x, 512 devices: a whole 4x4x16 slice. The times are simulated.
512 devices in a mesh: user: 32 (over x_lo, z), feat: 8 (over y, x_hi), dom: 2 (over core).
Axes of the slice: x: 4 (x_hi: 2, x_lo: 2; x = x_hi * 2 + x_lo), y: 4, z: 16, core: 2. Of those that a mesh axis runs over, the one named last changes fastest.
Arguments:
- side_matrix: bfloat16 [16384, 16384], P('user', ('feat', 'dom')), may hold values from -6 to 6
- slab: bfloat16 [8, 256, 16384], P('dom', 'feat', 'user'), may hold values from -6 to 6
- user_factor: bfloat16 [16384, 512], P('user'), may hold values from -6 to 6
- feat_factor: bfloat16 [512, 16384], P('user', ('feat', 'dom')), may hold values from -0.25 to 0.25
- item_factor: bfloat16 [256, 512], P('feat'), may hold values from -6 to 6
- domain_factor: bfloat16 [8, 512], P('dom'), may hold values from -0.25 to 0.25
Outputs:
- grad_user: float32 [16384, 512], P('user', ('feat', 'dom'))
- grad_feat: float32 [512, 16384], P('user', ('feat', 'dom'))
- grad_item: float32 [256, 512], P('feat')
- grad_domain: float32 [8, 512], P('dom')
All inputs are finite; a program needn't handle non-finite values.
Results may differ from a plain program's by a relative error of at most 0.0017.
Values may be sent and summed in bfloat16 or wider, within the bound.
A program may use at most 64 MiB of HBM per device.

v0:
```python
import math

import jax
import jax.numpy as jnp
from jax import lax
from jax.sharding import PartitionSpec as P

RANK = 512
FEATS = 16384
ITEMS = 256
DOMS = 8


def local(side_matrix, slab, user_factor, feat_factor, item_factor, domain_factor):
    users_total = user_factor.shape[0] * lax.axis_size("user")
    local_users = user_factor.shape[0]
    gathered_panel = lax.all_gather(feat_factor, "user", axis=0, tiled=True)
    domain_item = (
        domain_factor.astype(jnp.float32)[:, None, :] * item_factor.astype(jnp.float32)[None, :, :]
    ).astype(jnp.bfloat16)
    domain_item = domain_item.reshape(slab.shape[0] * slab.shape[1], RANK)
    tensor_model = jnp.dot(domain_item, user_factor.T, preferred_element_type=jnp.float32)
    tensor_res = (
        tensor_model - slab.reshape(slab.shape[0] * slab.shape[1], local_users).astype(jnp.float32)
    ).astype(jnp.bfloat16)
    tensor_user = jnp.dot(
        tensor_res.T, domain_item, preferred_element_type=jnp.float32
    ) * math.sqrt(RANK / (ITEMS * DOMS))
    projected = jnp.dot(tensor_res, user_factor, preferred_element_type=jnp.float32).reshape(
        slab.shape[0], slab.shape[1], RANK
    )
    item_term = math.sqrt(RANK / (users_total * DOMS)) * jnp.sum(
        projected * domain_factor.astype(jnp.float32)[:, None, :], axis=0
    )
    grad_item = lax.psum(item_term, ("user", "dom"))
    domain_term = jnp.sum(
        projected * item_factor.astype(jnp.float32)[None, :, :], axis=1
    ) / math.sqrt(users_total * ITEMS)
    grad_domain = lax.psum(domain_term, ("user", "feat"))
    side_model = jnp.dot(user_factor, gathered_panel, preferred_element_type=jnp.float32)
    side_res = (side_model - side_matrix.astype(jnp.float32)).astype(jnp.bfloat16)
    side_user = jnp.dot(side_res, gathered_panel.T, preferred_element_type=jnp.float32) * math.sqrt(
        RANK / FEATS
    )
    feat_scale = 1.0 / math.sqrt(users_total)
    grad_feat = lax.psum_scatter(
        jnp.dot(user_factor.T, side_res, preferred_element_type=jnp.float32) * feat_scale,
        "user",
        scatter_dimension=0,
        tiled=True,
    )
    side_share = lax.psum_scatter(side_user, ("feat", "dom"), scatter_dimension=1, tiled=True)
    tensor_share = lax.psum_scatter(tensor_user, ("feat", "dom"), scatter_dimension=1, tiled=True)
    grad_user = side_share + tensor_share
    return (grad_user, grad_feat, grad_item, grad_domain)


def solution(mesh):
    return jax.shard_map(
        local,
        mesh=mesh,
        in_specs=(
            P("user", ("feat", "dom")),
            P("dom", "feat", "user"),
            P("user", None),
            P("user", ("feat", "dom")),
            P("feat", None),
            P("dom", None),
        ),
        out_specs=(
            P("user", ("feat", "dom")),
            P("user", ("feat", "dom")),
            P("feat", None),
            P("dom", None),
        ),
        check_vma=False,
    )
```

profile of v0, /device:TPU:128, one launch (start us, length us, event | category | flops | bytes accessed | tf_op | source)
XLA Modules:
  0.0 876.1 jit_solution(4337313497104246148)
XLA Ops:
  8.0 0.0 copy-start
  8.0 0.0 copy-start.3
  8.0 0.0 all-gather.2.cloned.1.call-start
  8.1 0.7 all-gather.2.cloned.1.call-update
  8.8 0.0 all-reduce.2.cloned.1.call-start
  8.8 0.7 convert_element_type.32
  9.5 0.8 convert_element_type.33
  10.3 0.0 copy-done
  10.3 1.2 fusion.1
  11.5 0.2 multiply_reduce_fusion
  11.8 0.6 broadcast_multiply_fusion
  12.4 0.0 all-reduce.2.cloned.1.call-update
  12.5 0.0 reduce-scatter.5.cloned.1.call-start
  12.5 0.3 convolution_multiply_fusion
  12.9 128.4 %all-gather.2.cloned.1.call-done = bf16[512,1024]{1,0:T(8,128)(2,1)} async-done(((bf16[16,1024]{1,0:T(8,128)(2,1)}), bf16[512,1024]{1,0:T(8,128)(2,1)}) %all-gather.2.cloned.1.call-update) | async-done | bytes 1048592 | tf_op jit(solution)/shard_map/all_gather | solution.py:17
  141.2 0.0 copy-done.3
  141.3 0.0 copy-start.2
  141.3 2.0 subtract_convert_fusion
  143.3 0.0 copy-start.1
  143.3 1.0 copy-done.1
  144.3 0.0 copy-done.2
  144.3 1.7 fusion
  146.1 0.0 reduce-scatter.5.cloned.1.call-update
  146.1 0.0 reduce-scatter.7.cloned.1.call-start
  146.1 2.0 multiply_bitcast_fusion
  148.1 1.9 copy.12
  150.0 0.0 reduce-scatter.7.cloned.1.call-update
  150.0 717.5 %psum.15 = f32[4,512]{1,0:T(4,128)} all-reduce(f32[4,512]{1,0:T(4,128)S(1)} %broadcast_multiply_fusion.1), channel_id=1, replica_groups=mesh['user'=32,'feat'=8,'dom'=2] {'user','feat'}, use_global_device_ids=true, to_apply=%region_6.0 | all-reduce | flops 2048 | bytes 16384 | tf_op jit(solution)/shard_map/psum | solution.py:39
  867.5 0.0 all-reduce.2.cloned.1.call-done
  867.5 0.0 reduce-scatter.5.cloned.1.call-done
  867.5 0.0 reduce-scatter.7.cloned.1.call-done
  867.5 1.5 copy.15
  (3 shorter events, 0.0 us)
Async XLA Ops:
  8.0 2.3 copy-start
  8.0 133.2 %copy-start.3 = (bf16[512,1024]{1,0:T(8,128)(2,1)S(1)}, bf16[512,1024]{1,0:T(8,128)(2,1)}, u32[]{:S(2)}) copy-start(bf16[512,1024]{1,0:T(8,128)(2,1)} %param.6) | copy-start | bytes 3145732
  8.0 133.2 %all-gather.2.cloned.1.call-start = ((), (), s32[]{:S(2)}) async-start(), calls=%async_computation.2 | async-start | bytes 1081344 | tf_op jit(solution)/shard_map/all_gather | solution.py:17
  8.8 858.7 %all-reduce.2.cloned.1.call-start = ((), (), s32[]{:S(2)}) async-start(), calls=%async_computation.3 | async-start | bytes 131072 | tf_op jit(solution)/shard_map/psum | solution.py:35
  12.5 855.0 %reduce-scatter.5.cloned.1.call-start = ((), (), s32[]{:S(2)}) async-start(), calls=%async_computation.4 | async-start | bytes 1114112 | tf_op jit(solution)/shard_map/reduce_scatter | solution.py:52
  141.3 3.1 copy-start.2
  143.3 1.0 copy-start.1
  146.1 721.4 %reduce-scatter.7.cloned.1.call-start = ((), (), s32[]{:S(2)}) async-start(), calls=%async_computation.5 | async-start | bytes 2162688
Sparse Core Ops, SparseCore 0:
  10.9 130.2 all-gather.1
  146.5 88.2 reduce-scatter.4
  238.4 131.2 reduce-scatter.6
Sparse Core Ops, SparseCore 1:
  12.7 375.2 all-reduce.1
where the time goes:
time: 876 us
  blocking collectives  717 us (82%)
  waiting for transfers between devices  129 us (15%)
  between operations  15.3 us (2%)
    psum x1, blocking collectives, local(): grad_domain = lax.psum(domain_term, ('user', 'feat'))  717 us
    all_gather x1, waiting for transfers between devices, local(): gathered_panel = lax.all_gather(feat_factor, 'user', axis=0, tiled=True)  128 us
  transfers between devices with their start and end apart: 4, of which 1 were waited for; matrix products, arithmetic and copies ran while one was open for 1% of the time, Pallas kernels for 0%

commit v1 on v0

v1 whole, which is shorter than its diff:
```python
import math

import jax
import jax.numpy as jnp
from jax import lax
from jax.experimental import pallas as pl
from jax.experimental.pallas import tpu as pltpu
from jax.sharding import PartitionSpec as P

MESH = pl.DeviceIdType.MESH
F32, BF16 = jnp.float32, jnp.bfloat16

RANK = 512
FEATS = 16384
ITEMS = 256
DOMS = 8
USERS = 16384

NZ = 16
ROWS = 16
CHUNKS = 2
HUBS = (0, 3, -3, 6, -6)
SLOTS = HUBS + tuple(h - 1 for h in HUBS) + tuple(h + 1 for h in HUBS) + (8,)

SIDE_SCALE = math.sqrt(RANK / FEATS)
TENSOR_SCALE = math.sqrt(RANK / (ITEMS * DOMS))
FEAT_SCALE = 1.0 / math.sqrt(USERS)
ITEM_SCALE = math.sqrt(RANK / (USERS * DOMS))
DOMAIN_SCALE = 1.0 / math.sqrt(USERS * ITEMS)

N_MESSAGES = 96
N_LOCAL = 8


def dot(a, b, ca=1, cb=0):
    return lax.dot_general(a, b, (((ca,), (cb,)), ((), ())), preferred_element_type=F32)


def kernel(
    side_h, slab_h, user_h, feat_h, item_h, domain_h,
    gu_ref, gf_ref, gi_ref, gd_ref,
    side, slab, user, items, domains,
    panel, user_rel, ut_abs, ut_rel,
    model_di, tensor_res, small, small_abs, tensor_user, side_user,
    gf_other, gf_own, gf_x, gf_send, gf_near, gf_far8, gf_hub, gf_far,
    sx_other, sx_own, sx_x, sx_send, sx_near, sx_far8, sx_hub, sx_far,
    row_send, row_recv, small_panel,
    su_all, su_core, su_core_recv, su_sum, su_send, su_recv,
    send_sems, recv_sems, local_sems,
):
    u, f, d = lax.axis_index("user"), lax.axis_index("feat"), lax.axis_index("dom")
    xl, z = u // NZ, u % NZ
    width = panel.shape[-1]

    def along(dz=0, dx=0):
        return ((xl + dx) % 2 * NZ + (z + dz + NZ) % NZ, f, d)

    def across(df):
        return (u, (f + df) % 8, d)

    partner = (u, f, 1 - d)
    counter = [0]

    def send(src, dst, device):
        i = counter[0]
        counter[0] += 1
        copy = pltpu.make_async_remote_copy(
            src, dst, send_sems.at[i], recv_sems.at[i], device_id=device, device_id_type=MESH
        )
        copy.start()
        sent.append(copy)
        return copy

    sent = []

    feat_copies = [
        pltpu.make_async_copy(
            feat_h.at[:, pl.ds(c * width, width)], panel.at[c, 0, 0], local_sems.at[c]
        )
        for c in range(CHUNKS)
    ]
    user_copy = pltpu.make_async_copy(user_h, user, local_sems.at[CHUNKS])
    item_copy = pltpu.make_async_copy(item_h, items, local_sems.at[CHUNKS + 1])
    domain_copy = pltpu.make_async_copy(domain_h, domains, local_sems.at[CHUNKS + 2])
    slab_copy = pltpu.make_async_copy(slab_h, slab, local_sems.at[CHUNKS + 3])
    side_copy = pltpu.make_async_copy(side_h, side, local_sems.at[CHUNKS + 4])
    for copy in feat_copies + [user_copy, item_copy, domain_copy, slab_copy, side_copy]:
        copy.start()

    barrier = pltpu.get_barrier_semaphore()
    greet = [along(dz) for dz in (1, -1, 2, -2, 3, -3, 6, -6)] + [along(0, 1), partner]
    greet += [across(df) for df in range(1, 8)]
    for device in greet:
        pl.semaphore_signal(barrier, inc=1, device_id=device, device_id_type=MESH)
    pl.semaphore_wait(barrier, len(greet))

    def gather_start(g):
        far = [send(g.at[0, 0], g.at[0, h], along(-HUBS[h])) for h in range(1, 5)]
        near = [send(g.at[0, 0], g.at[0, 5], along(1)), send(g.at[0, 0], g.at[0, 10], along(-1))]
        other = [send(g.at[0, 0], g.at[1, 0], along(0, 1))]
        return far, near, other

    def gather_near(g, state):
        far, near, other = state
        for lo in (1, 3):
            for copy in far[lo - 1 : lo + 1]:
                copy.wait_recv()
            two = pl.ds(lo, 2)
            near.append(send(g.at[0, two], g.at[0, pl.ds(5 + lo, 2)], along(1)))
            near.append(send(g.at[0, two], g.at[0, pl.ds(10 + lo, 2)], along(-1)))
        near.append(send(g.at[0, 3], g.at[0, 15], along(-2)))
        other.append(send(g.at[0, pl.ds(1, 4)], g.at[1, pl.ds(1, 4)], along(0, 1)))

    def gather_other(g, state):
        far, near, other = state
        for copy in near:
            copy.wait_recv()
        other.append(send(g.at[0, pl.ds(5, 11)], g.at[1, pl.ds(5, 11)], along(0, 1)))

    def gather_end(state):
        for copy in state[2]:
            copy.wait_recv()

    def reduce_near(own, x, stage, near, far8, state):
        for copy in state:
            copy.wait_recv()
        stage[...] = (own[5:] + x[5:].astype(F32)).astype(BF16)
        copies = [
            send(stage.at[pl.ds(5, 5)], near.at[0], along(1)),
            send(stage.at[pl.ds(0, 5)], near.at[1], along(-1)),
            send(stage.at[10], far8, along(2)),
        ]
        own[:5] = own[:5] + x[:5].astype(F32)
        return copies

    def reduce_far(own, near, far8, hub, far, state):
        for copy in state:
            copy.wait_recv()
        own[:5] = own[:5] + near[0].astype(F32) + near[1].astype(F32)
        own[3] = own[3] + far8[...].astype(F32)
        hub[...] = own[1:5].astype(BF16)
        return [send(hub.at[h - 1], far.at[h - 1], along(HUBS[h])) for h in range(1, 5)]

    def reduce_end(own, far, state):
        for copy in state:
            copy.wait_recv()
        total = own[0]
        for h in range(4):
            total = total + far[h].astype(F32)
        return total

    gathers = []
    for c in range(CHUNKS):
        feat_copies[c].wait()
        gathers.append(gather_start(panel.at[c]))

    def absolute(plane, slot):
        return (xl + plane) % 2 * NZ + (z + SLOTS[slot] + NZ) % NZ

    user_copy.wait()
    item_copy.wait()
    domain_copy.wait()
    slab_copy.wait()
    for k in range(4):
        model_di[32 * k : 32 * k + 32, :] = (
            domains[k : k + 1, :].astype(F32) * items[...].astype(F32)
        ).astype(BF16)
    tensor_res[...] = (
        dot(model_di[...], user[...], 1, 1) - slab[...].reshape(128, 512).astype(F32)
    ).astype(BF16)
    projected = dot(tensor_res[...], user[...])
    item_term = jnp.zeros((32, RANK), F32)
    small[...] = jnp.zeros_like(small)
    for k in range(4):
        part = projected[32 * k : 32 * k + 32, :]
        item_term = item_term + part * domains[k : k + 1, :].astype(F32)
        small[32 + k : 33 + k, :] = DOMAIN_SCALE * jnp.sum(
            part * items[...].astype(F32), axis=0, keepdims=True
        )
    small[0:32, :] = ITEM_SCALE * item_term
    small_abs[...] = small[...].T.reshape(32, ROWS, 128)
    for slot in range(NZ):
        sx_other[slot] = small_abs[absolute(1, slot)].astype(BF16)
        sx_own[slot] = small_abs[absolute(0, slot)]
    sx_state = [send(sx_other, sx_x, along(0, 1))]

    ut_abs[...] = user[...].T.reshape(32, ROWS, 512)
    for plane in range(2):
        for slot in range(NZ):
            ut_rel[plane, slot] = ut_abs[absolute(plane, slot)]
    user_rel[...] = ut_rel[...].reshape(512, 512).T

    gather_near(panel.at[0], gathers[0])
    tensor_user[...] = (
        TENSOR_SCALE * dot(model_di[...], tensor_res[...], 0, 0)
    ).reshape(32, ROWS, 512)
    gather_near(panel.at[1], gathers[1])
    sx_state = reduce_near(sx_own, sx_x, sx_send, sx_near, sx_far8, sx_state)
    gather_other(panel.at[0], gathers[0])
    gather_other(panel.at[1], gathers[1])
    sx_state = reduce_far(sx_own, sx_near, sx_far8, sx_hub, sx_far, sx_state)

    side_copy.wait()
    gf_state = []

    def compute(c):
        gather_end(gathers[c])
        block = panel[c].reshape(512, width)
        res = (
            dot(user_rel[...], block) - side[:, c * width : (c + 1) * width].astype(F32)
        ).astype(BF16)
        gf_other[c] = dot(ut_rel[1].reshape(256, 512), res).reshape(NZ, ROWS, width).astype(BF16)
        gf_state.append([send(gf_other.at[c], gf_x.at[c], along(0, 1))])
        gf_own[c] = dot(ut_rel[0].reshape(256, 512), res).reshape(NZ, ROWS, width)
        part = dot(block, res, 1, 1).reshape(32, ROWS, 512)
        if c == 0:
            side_user[...] = part
        else:
            side_user[...] = side_user[...] + part

    compute(0)

    total = reduce_end(sx_own, sx_far, sx_state)
    row_send[...] = total
    row_copies = [send(row_send, row_recv.at[0], partner)]
    row_copies += [send(row_send, row_recv.at[df], across(df)) for df in range(1, 8)]

    compute(1)

    for plane in range(2):
        for slot in range(NZ):
            b = absolute(plane, slot)
            place = (b // 2 + d) % 2 * 16 + b // 4 * 2 + b % 2
            su_all[place] = SIDE_SCALE * side_user[plane * NZ + slot] + tensor_user[b]
    su_core[...] = su_all[16:].astype(BF16)
    su_copy = send(su_core, su_core_recv, partner)

    def gf_near_step(c):
        gf_state[c] = reduce_near(
            gf_own.at[c], gf_x.at[c], gf_send.at[c], gf_near.at[c], gf_far8.at[c], gf_state[c]
        )

    def gf_far_step(c):
        gf_state[c] = reduce_far(
            gf_own.at[c], gf_near.at[c], gf_far8.at[c], gf_hub.at[c], gf_far.at[c], gf_state[c]
        )

    gf_near_step(0)
    for copy in row_copies:
        copy.wait_recv()
    lane = lax.broadcasted_iota(jnp.int32, (ROWS, 128), 1)
    feats = row_recv[1]
    for df in range(2, 8):
        feats = feats + row_recv[df]
    small_panel[0, 0] = total + jnp.where(lane < 32, row_recv[0], feats)
    small_gather = gather_start(small_panel)

    gf_near_step(1)
    su_copy.wait_recv()
    su_sum[...] = (su_all[:16] + su_core_recv[...].astype(F32)).reshape(8, 32, 512)
    su_send[...] = su_sum[...].astype(BF16)
    su_copies = [
        send(su_send.at[(f + df) % 8], su_recv.at[df - 1], across(df)) for df in range(1, 8)
    ]
    gf_far_step(0)
    gather_near(small_panel, small_gather)
    gf_far_step(1)
    gather_other(small_panel, small_gather)

    gf_ref[:, 0:width] = FEAT_SCALE * reduce_end(gf_own.at[0], gf_far.at[0], gf_state[0])
    for copy in su_copies:
        copy.wait_recv()
    grad = su_sum[f]
    for df in range(7):
        grad = grad + su_recv[df].astype(F32)
    gu_ref[...] = grad
    gather_end(small_gather)
    for plane in range(2):
        for slot in range(NZ):
            small_abs[absolute(plane, slot)] = small_panel[plane, slot]
    small[...] = small_abs[...].reshape(512, 128).T
    gi_ref[...] = small[0:32, :]
    gd_ref[...] = small[32:36, :]
    gf_ref[:, width:] = FEAT_SCALE * reduce_end(gf_own.at[1], gf_far.at[1], gf_state[1])
    for copy in sent:
        copy.wait_send()


def local(side_matrix, slab, user_factor, feat_factor, item_factor, domain_factor):
    width = 1024 // CHUNKS

    def reduction(lead, w):
        return [
            pltpu.VMEM(lead + (NZ, ROWS, w), BF16),
            pltpu.VMEM(lead + (NZ, ROWS, w), F32),
            pltpu.VMEM(lead + (NZ, ROWS, w), BF16),
            pltpu.VMEM(lead + (11, ROWS, w), BF16),
            pltpu.VMEM(lead + (2, 5, ROWS, w), BF16),
            pltpu.VMEM(lead + (ROWS, w), BF16),
            pltpu.VMEM(lead + (4, ROWS, w), BF16),
            pltpu.VMEM(lead + (4, ROWS, w), BF16),
        ]

    grad_user, grad_feat, grad_item, grad_domain = pl.pallas_call(
        kernel,
        out_shape=(
            jax.ShapeDtypeStruct((32, 512), F32),
            jax.ShapeDtypeStruct((ROWS, 1024), F32),
            jax.ShapeDtypeStruct((32, RANK), F32),
            jax.ShapeDtypeStruct((4, RANK), F32),
        ),
        in_specs=[pl.BlockSpec(memory_space=pl.ANY)] * 6,
        out_specs=[pl.BlockSpec(memory_space=pltpu.VMEM)] * 4,
        scratch_shapes=[
            pltpu.VMEM((512, 1024), BF16),
            pltpu.VMEM((4, 32, 512), BF16),
            pltpu.VMEM((512, 512), BF16),
            pltpu.VMEM((32, 512), BF16),
            pltpu.VMEM((4, 512), BF16),
            pltpu.VMEM((CHUNKS, 2, NZ, ROWS, width), BF16),
            pltpu.VMEM((512, 512), BF16),
            pltpu.VMEM((32, ROWS, 512), BF16),
            pltpu.VMEM((2, NZ, ROWS, 512), BF16),
            pltpu.VMEM((128, 512), BF16),
            pltpu.VMEM((128, 512), BF16),
            pltpu.VMEM((128, 512), F32),
            pltpu.VMEM((32, ROWS, 128), F32),
            pltpu.VMEM((32, ROWS, 512), F32),
            pltpu.VMEM((32, ROWS, 512), F32),
        ]
        + reduction((CHUNKS,), width)
        + reduction((), 128)
        + [
            pltpu.VMEM((ROWS, 128), F32),
            pltpu.VMEM((8, ROWS, 128), F32),
            pltpu.VMEM((2, NZ, ROWS, 128), F32),
            pltpu.VMEM((32, ROWS, 512), F32),
            pltpu.VMEM((16, ROWS, 512), BF16),
            pltpu.VMEM((16, ROWS, 512), BF16),
            pltpu.VMEM((8, 32, 512), F32),
            pltpu.VMEM((8, 32, 512), BF16),
            pltpu.VMEM((7, 32, 512), BF16),
            pltpu.SemaphoreType.DMA((N_MESSAGES,)),
            pltpu.SemaphoreType.DMA((N_MESSAGES,)),
            pltpu.SemaphoreType.DMA((N_LOCAL,)),
        ],
        compiler_params=pltpu.CompilerParams(
            collective_id=0, has_side_effects=True, vmem_limit_bytes=48 << 20
        ),
        name="factor_gradients",
    )(side_matrix, slab, user_factor, feat_factor, item_factor, domain_factor)
    return grad_user.T, grad_feat, grad_item, grad_domain


def solution(mesh):
    return jax.shard_map(
        local,
        mesh=mesh,
        in_specs=(
            P("user", ("feat", "dom")),
            P("dom", "feat", "user"),
            P("user", None),
            P("user", ("feat", "dom")),
            P("feat", None),
            P("dom", None),
        ),
        out_specs=(
            P("user", ("feat", "dom")),
            P("user", ("feat", "dom")),
            P("feat", None),
            P("dom", None),
        ),
        check_vma=False,
    )
```

time: 876 us -> 72 us (0.08)
  the two profiles are of different devices: /device:TPU:128 before, /device:TPU:24 now
where the time goes in v1:
time: 72 us; the launch traced here: 71.2 us
  Pallas kernels  62.7 us (87%)
  local copies, waits for them, and re-layouts  7.85 us (11%)
    pallas_call x1, Pallas kernels, local(): pl.pallas_call(kernel, out_shape=(jax.ShapeDtypeStruct((32, 512), F32), j...  62.7 us
    unnamed x16, local copies, waits for them, and re-layouts  7.85 us

profile of v1, /device:TPU:24, one launch (start us, length us, event | category | flops | bytes accessed | tf_op | source)
XLA Modules:
  0.0 71.2 jit_solution(16777879035707262938)
XLA Ops:
  0.6 0.0 copy-start
  0.6 1.2 %copy-done = bf16[512,1024]{1,0:T(8,128)(2,1)S(1)} copy-done((bf16[512,1024]{1,0:T(8,128)(2,1)S(1)}, bf16[512,1024]{1,0:T(8,128)(2,1)}, u32[]{:S(2)}) %copy-start) | copy-done | bytes 1048600
  1.9 0.0 copy-start.1
  1.9 1.0 %copy-done.1 = bf16[512,512]{1,0:T(8,128)(2,1)S(1)} copy-done((bf16[512,512]{1,0:T(8,128)(2,1)S(1)}, bf16[512,512]{1,0:T(8,128)(2,1)}, u32[]{:S(2)}) %copy-start.1) | copy-done | bytes 524312
  2.9 0.0 copy-start.2
  2.9 0.9 %copy-done.2 = bf16[4,32,512]{2,1,0:T(8,128)(2,1)S(1)} copy-done((bf16[4,32,512]{2,1,0:T(8,128)(2,1)S(1)}, bf16[4,32,512]{2,1,0:T(8,128)(2,1)}, u32[]{:S(2)}) %copy-start.2) | copy-done | bytes 131096
  3.8 0.0 copy-start.3
  3.8 0.8 %copy-done.3 = bf16[16,1024]{1,0:T(8,128)(2,1)S(1)} copy-done((bf16[16,1024]{1,0:T(8,128)(2,1)S(1)}, bf16[16,1024]{1,0:T(8,128)(2,1)}, u32[]{:S(2)}) %copy-start.3) | copy-done | bytes 32792
  4.6 0.0 copy-start.4
  4.6 0.8 %copy-done.4 = bf16[32,512]{1,0:T(8,128)(2,1)S(1)} copy-done((bf16[32,512]{1,0:T(8,128)(2,1)S(1)}, bf16[32,512]{1,0:T(8,128)(2,1)}, u32[]{:S(2)}) %copy-start.4) | copy-done | bytes 32792
  5.3 0.0 copy-start.5
  5.3 0.7 copy-done.5
  6.0 62.7 %factor_gradients.1 = (f32[32,512]{1,0:T(8,128)S(1)}, f32[16,1024]{1,0:T(8,128)S(1)}, f32[32,512]{1,0:T(8,128)S(1)}, f32[4,512]{1,0:T(4,128)S(1)}) custom-call(bf16[512,1024]{1,0:T(8,128)(2,1)S(1)} %copy-done, bf16[4,32,512]{2,1,0:T(8,128)(2,1)S(1)} %copy-done.2, bf16[512,512]{1,0:T(8,128)(2,1)S(1)} %copy-done.1, bf16[16,1024]{1,0:T(8,128)(2,1)S(1)} %copy-done.3, ...), custom_call_target="tpu_custom_call" | custom-call | tf_op jit(solution)/shard_map/factor_gradients/pallas_call | solution.py:304
  68.7 0.6 copy.14
  69.4 0.6 copy.15
  70.0 0.6 copy.16
  70.6 0.6 copy.17
Async XLA Ops:
  0.6 1.2 %copy-start = (bf16[512,1024]{1,0:T(8,128)(2,1)S(1)}, bf16[512,1024]{1,0:T(8,128)(2,1)}, u32[]{:S(2)}) copy-start(bf16[512,1024]{1,0:T(8,128)(2,1)} %side_h.1) | copy-start | bytes 3145732
  1.9 1.0 %copy-start.1 = (bf16[512,512]{1,0:T(8,128)(2,1)S(1)}, bf16[512,512]{1,0:T(8,128)(2,1)}, u32[]{:S(2)}) copy-start(bf16[512,512]{1,0:T(8,128)(2,1)} %user_h.1) | copy-start | bytes 1572868
  2.9 0.9 %copy-start.2 = (bf16[4,32,512]{2,1,0:T(8,128)(2,1)S(1)}, bf16[4,32,512]{2,1,0:T(8,128)(2,1)}, u32[]{:S(2)}) copy-start(bf16[4,32,512]{2,1,0:T(8,128)(2,1)} %slab_h.1) | copy-start | bytes 393220
  3.8 0.8 %copy-start.3 = (bf16[16,1024]{1,0:T(8,128)(2,1)S(1)}, bf16[16,1024]{1,0:T(8,128)(2,1)}, u32[]{:S(2)}) copy-start(bf16[16,1024]{1,0:T(8,128)(2,1)} %feat_h.1) | copy-start | bytes 98308
  4.6 0.8 %copy-start.4 = (bf16[32,512]{1,0:T(8,128)(2,1)S(1)}, bf16[32,512]{1,0:T(8,128)(2,1)}, u32[]{:S(2)}) copy-start(bf16[32,512]{1,0:T(8,128)(2,1)} %item_h.1) | copy-start | bytes 98308
  5.3 0.7 copy-start.5

commit v2 on v1

v2 whole, which is shorter than its diff:
```python
import math

import jax
import jax.numpy as jnp
from jax import lax
from jax.experimental import pallas as pl
from jax.experimental.pallas import tpu as pltpu
from jax.sharding import PartitionSpec as P

MESH = pl.DeviceIdType.MESH
F32, BF16 = jnp.float32, jnp.bfloat16

RANK = 512
FEATS = 16384
ITEMS = 256
DOMS = 8
USERS = 16384

NZ = 16
ROWS = 16
CHUNKS = 2
HUBS = (0, 3, -3, 6, -6)
SLOTS = tuple(h + j for h in HUBS for j in (0, -1, 1)) + (8,)

SIDE_SCALE = math.sqrt(RANK / FEATS)
TENSOR_SCALE = math.sqrt(RANK / (ITEMS * DOMS))
FEAT_SCALE = 1.0 / math.sqrt(USERS)
ITEM_SCALE = math.sqrt(RANK / (USERS * DOMS))
DOMAIN_SCALE = 1.0 / math.sqrt(USERS * ITEMS)

N_MESSAGES = 128
N_LOCAL = 8


def dot(a, b, ca=1, cb=0):
    return lax.dot_general(a, b, (((ca,), (cb,)), ((), ())), preferred_element_type=F32)


def kernel(
    side_h, slab_h, user_h, feat_h, item_h, domain_h,
    gu_ref, gf_ref, gi_ref, gd_ref,
    side, slab, user, items, domains,
    panel, user_rel, ut_abs, ut_rel,
    model_di, tensor_res, small, small_abs, tensor_user, side_user,
    gf_other, gf_own, gf_x, gf_send, gf_near, gf_hub, gf_far,
    sx_other, sx_own, sx_x, sx_send, sx_near, sx_hub, sx_far,
    row_send, row_recv, row_y, small_panel,
    su_all, su_core, su_core_recv, su_sum, su_send, su_recv, su_y, su_x,
    send_sems, recv_sems, local_sems,
):
    u, f, d = lax.axis_index("user"), lax.axis_index("feat"), lax.axis_index("dom")
    xl, z, y, xh = u // NZ, u % NZ, f // 2, f % 2
    width = panel.shape[-1]

    def along(dz=0, dx=0):
        return ((xl + dx) % 2 * NZ + (z + dz + NZ) % NZ, f, d)

    def beside(dy):
        return (u, (y + dy) % 4 * 2 + xh, d)

    partner, opposite = (u, f, 1 - d), (u, y * 2 + 1 - xh, d)
    counter = [0]

    def send(src, dst, device):
        i = counter[0]
        counter[0] += 1
        copy = pltpu.make_async_remote_copy(
            src, dst, send_sems.at[i], recv_sems.at[i], device_id=device, device_id_type=MESH
        )
        copy.start()
        sent.append(copy)
        return copy

    sent = []

    feat_copies = [
        pltpu.make_async_copy(
            feat_h.at[:, pl.ds(c * width, width)], panel.at[c, 0, 0, 0], local_sems.at[c]
        )
        for c in range(CHUNKS)
    ]
    user_copy = pltpu.make_async_copy(user_h, user, local_sems.at[CHUNKS])
    item_copy = pltpu.make_async_copy(item_h, items, local_sems.at[CHUNKS + 1])
    domain_copy = pltpu.make_async_copy(domain_h, domains, local_sems.at[CHUNKS + 2])
    slab_copy = pltpu.make_async_copy(slab_h, slab, local_sems.at[CHUNKS + 3])
    side_copy = pltpu.make_async_copy(side_h, side, local_sems.at[CHUNKS + 4])
    for copy in feat_copies + [user_copy, item_copy, domain_copy, slab_copy, side_copy]:
        copy.start()

    barrier = pltpu.get_barrier_semaphore()
    greet = [along(dz) for dz in (1, -1, 2, -2, 3, -3)] + [along(0, 1), partner]
    greet += [beside(dy) for dy in range(1, 4)] + [opposite]
    for device in greet:
        pl.semaphore_signal(barrier, inc=1, device_id=device, device_id_type=MESH)
    pl.semaphore_wait(barrier, len(greet))

    def gather_start(g):
        own = g.at[0, 0, 0]
        far = [send(own, g.at[0, h, 0], along(-HUBS[h])) for h in (1, 2)]
        near = [send(own, g.at[0, 0, 1], along(1)), send(own, g.at[0, 0, 2], along(-1))]
        return {"far": far, "near": near, "other": []}

    def gather_own(g, state):
        for copy in state["near"]:
            copy.wait_recv()
        state["other"].append(send(g.at[0, 0], g.at[1, 0], along(0, 1)))

    def gather_hubs(g, state, lo):
        for copy in state["far"]:
            copy.wait_recv()
        if lo == 1:
            state["far"] = [
                send(g.at[0, h, 0], g.at[0, h + 2, 0], along(-HUBS[h])) for h in (1, 2)
            ]
        two = pl.ds(lo, 2)
        hub = g.at[0, two, 0]
        state["near"] = [send(hub, g.at[0, two, 1], along(1)), send(hub, g.at[0, two, 2], along(-1))]
        if lo == 3:
            state["near"].append(send(g.at[0, 3, 0], g.at[0, 5, 0], along(-2)))
            state["other"].append(send(hub, g.at[1, two, 0], along(0, 1)))

    def gather_near(g, state, lo):
        for copy in state["near"]:
            copy.wait_recv()
        two = pl.ds(lo, 2)
        if lo == 3:
            rest = pl.ds(1, 2)
            state["other"].append(send(g.at[0, two, rest], g.at[1, two, rest], along(0, 1)))
            state["other"].append(send(g.at[0, 5, 0], g.at[1, 5, 0], along(0, 1)))
        else:
            state["other"].append(send(g.at[0, two], g.at[1, two], along(0, 1)))

    def gather_end(state):
        for copy in state["other"]:
            copy.wait_recv()

    groups = ((9, 16), (3, 9), (0, 3))

    def reduce_start(other, x):
        parts = [pl.ds(lo, hi - lo) for lo, hi in groups]
        return {"x": [send(other.at[p], x.at[p], along(0, 1)) for p in parts], "near": {}, "far": []}

    def reduce_near(own, x, stage, near, state, i):
        lo, hi = groups[i]
        state["x"][i].wait_recv()
        total = own[lo:hi] + x[lo:hi].astype(F32)
        own[lo:hi] = total
        first, count = lo // 3, (hi - lo) // 3
        for h in range(count):
            stage[first + h] = total[3 * h : 3 * h + 3].astype(BF16)
        some = pl.ds(first, count)
        state["near"][i] = [
            send(stage.at[some, 2], near.at[some, 2], along(1)),
            send(stage.at[some, 1], near.at[some, 1], along(-1)),
        ]
        if i == 0:
            stage[5, 0] = total[6].astype(BF16)
            state["near"][i].append(send(stage.at[5, 0], near.at[5, 0], along(2)))

    def reduce_far(own, near, hub, far, state, i):
        for copy in state["near"][i]:
            copy.wait_recv()
        lo, hi = groups[i]
        for h in range(lo // 3, lo // 3 + (hi - lo) // 3):
            total = own[3 * h] + near[h, 1].astype(F32) + near[h, 2].astype(F32)
            if h == 3:
                total = total + near[5, 0].astype(F32)
            if h == 0:
                own[0] = total
            else:
                hub[h - 1] = total.astype(BF16)
                state["far"].append(send(hub.at[h - 1], far.at[h - 1], along(HUBS[h])))

    def reduce_end(own, far, state):
        for copy in state["far"]:
            copy.wait_recv()
        total = own[0]
        for h in range(4):
            total = total + far[h].astype(F32)
        return total

    gathers = []
    for c in range(CHUNKS):
        feat_copies[c].wait()
        gathers.append(gather_start(panel.at[c]))

    def absolute(plane, slot):
        return (xl + plane) % 2 * NZ + (z + SLOTS[slot] + NZ) % NZ

    user_copy.wait()
    item_copy.wait()
    domain_copy.wait()
    slab_copy.wait()
    for k in range(4):
        model_di[32 * k : 32 * k + 32, :] = (
            domains[k : k + 1, :].astype(F32) * items[...].astype(F32)
        ).astype(BF16)
    tensor_res[...] = (
        dot(model_di[...], user[...], 1, 1) - slab[...].reshape(128, 512).astype(F32)
    ).astype(BF16)
    projected = dot(tensor_res[...], user[...])
    item_term = jnp.zeros((32, RANK), F32)
    small[...] = jnp.zeros_like(small)
    for k in range(4):
        part = projected[32 * k : 32 * k + 32, :]
        item_term = item_term + part * domains[k : k + 1, :].astype(F32)
        small[32 + k : 33 + k, :] = DOMAIN_SCALE * jnp.sum(
            part * items[...].astype(F32), axis=0, keepdims=True
        )
    small[0:32, :] = ITEM_SCALE * item_term
    small_abs[...] = small[...].T.reshape(32, ROWS, 128)
    for slot in range(NZ):
        sx_other[slot] = small_abs[absolute(1, slot)].astype(BF16)
        sx_own[slot] = small_abs[absolute(0, slot)]
    sx_state = reduce_start(sx_other, sx_x)

    ut_abs[...] = user[...].T.reshape(32, ROWS, 512)
    for plane in range(2):
        for slot in range(NZ):
            ut_rel[plane, slot] = ut_abs[absolute(plane, slot)]
    user_rel[...] = ut_rel[...].reshape(512, 512).T
    tensor_user[...] = (
        TENSOR_SCALE * dot(model_di[...], tensor_res[...], 0, 0)
    ).reshape(32, ROWS, 512)

    for c in range(CHUNKS):
        gather_own(panel.at[c], gathers[c])
    for i in range(3):
        reduce_near(sx_own, sx_x, sx_send, sx_near, sx_state, i)
    for c in range(CHUNKS):
        gather_hubs(panel.at[c], gathers[c], 1)
    for i in range(3):
        reduce_far(sx_own, sx_near, sx_hub, sx_far, sx_state, i)
    for c in range(CHUNKS):
        gather_near(panel.at[c], gathers[c], 1)
    for c in range(CHUNKS):
        gather_hubs(panel.at[c], gathers[c], 3)
    for c in range(CHUNKS):
        gather_near(panel.at[c], gathers[c], 3)

    total = reduce_end(sx_own, sx_far, sx_state)
    row_send[...] = total
    row_copies = [send(row_send, row_recv.at[0], partner)]
    row_copies += [send(row_send, row_recv.at[dy], beside(dy)) for dy in range(1, 4)]

    side_copy.wait()
    gf_state = []

    def compute(c):
        gather_end(gathers[c])
        blocks = [panel[c, p].reshape(18 * ROWS, width)[0:256] for p in range(2)]
        model = dot(user_rel[:, 0:256], blocks[0]) + dot(user_rel[:, 256:512], blocks[1])
        res = (model - side[:, c * width : (c + 1) * width].astype(F32)).astype(BF16)
        gf_other[c] = dot(ut_rel[1].reshape(256, 512), res).reshape(NZ, ROWS, width).astype(BF16)
        gf_state.append(reduce_start(gf_other.at[c], gf_x.at[c]))
        gf_own[c] = dot(ut_rel[0].reshape(256, 512), res).reshape(NZ, ROWS, width)
        for p in range(2):
            part = dot(blocks[p], res, 1, 1).reshape(NZ, ROWS, 512)
            side_user[p] = part if c == 0 else side_user[p] + part

    compute(0)
    compute(1)

    for copy in row_copies:
        copy.wait_recv()
    lane = lax.broadcasted_iota(jnp.int32, (ROWS, 128), 1)
    row_y[...] = row_send[...] + row_recv[1] + row_recv[2] + row_recv[3]
    row_copy = send(row_y, row_recv.at[4], opposite)

    for plane in range(2):
        for slot in range(NZ):
            b = absolute(plane, slot)
            place = (b // 2 + d) % 2 * 16 + b // 4 * 2 + b % 2
            su_all[place] = SIDE_SCALE * side_user[plane, slot] + tensor_user[b]
    su_core[...] = su_all[16:].astype(BF16)
    su_copy = send(su_core, su_core_recv, partner)

    def gf_near_step(c, i):
        reduce_near(gf_own.at[c], gf_x.at[c], gf_send.at[c], gf_near.at[c], gf_state[c], i)

    def gf_far_step(c, i):
        reduce_far(gf_own.at[c], gf_near.at[c], gf_hub.at[c], gf_far.at[c], gf_state[c], i)

    gf_near_step(0, 0)
    su_copy.wait_recv()
    su_sum[...] = (su_all[:16] + su_core_recv[...].astype(F32)).reshape(8, 32, 512)
    su_send[...] = su_sum[...].astype(BF16)
    su_copies = [
        send(su_send.at[pl.ds((y + dy) % 4 * 2, 2)], su_recv.at[dy - 1], beside(dy))
        for dy in range(1, 4)
    ]
    gf_near_step(0, 1)
    row_copy.wait_recv()
    small_panel[0, 0, 0] = jnp.where(
        lane < 32, row_send[...] + row_recv[0], row_y[...] + row_recv[4]
    )
    small_gather = gather_start(small_panel)
    gf_near_step(0, 2)
    gf_far_step(0, 0)
    gf_near_step(1, 0)
    gather_own(small_panel, small_gather)
    gf_far_step(0, 1)
    gf_near_step(1, 1)
    for copy in su_copies:
        copy.wait_recv()
    for i in range(2):
        grad = su_sum[y * 2 + i]
        for dy in range(3):
            grad = grad + su_recv[dy, i].astype(F32)
        su_y[i] = grad
    su_copy = send(su_y.at[1 - xh], su_x, opposite)
    gf_far_step(1, 0)
    gf_near_step(1, 2)
    gather_hubs(small_panel, small_gather, 1)
    gf_far_step(1, 1)
    gf_far_step(0, 2)
    gf_far_step(1, 2)
    gather_near(small_panel, small_gather, 1)
    gather_hubs(small_panel, small_gather, 3)
    gather_near(small_panel, small_gather, 3)

    su_copy.wait_recv()
    gu_ref[...] = su_y[xh] + su_x[...]
    gf_ref[:, 0:width] = FEAT_SCALE * reduce_end(gf_own.at[0], gf_far.at[0], gf_state[0])
    gf_ref[:, width:] = FEAT_SCALE * reduce_end(gf_own.at[1], gf_far.at[1], gf_state[1])
    gather_end(small_gather)
    for plane in range(2):
        for slot in range(NZ):
            small_abs[absolute(plane, slot)] = small_panel[plane, slot // 3, slot % 3]
    small[...] = small_abs[...].reshape(512, 128).T
    gi_ref[...] = small[0:32, :]
    gd_ref[...] = small[32:36, :]
    for copy in sent:
        copy.wait_send()


def local(side_matrix, slab, user_factor, feat_factor, item_factor, domain_factor):
    width = 1024 // CHUNKS

    def reduction(lead, w):
        return [
            pltpu.VMEM(lead + (NZ, ROWS, w), BF16),
            pltpu.VMEM(lead + (NZ, ROWS, w), F32),
            pltpu.VMEM(lead + (NZ, ROWS, w), BF16),
            pltpu.VMEM(lead + (6, 3, ROWS, w), BF16),
            pltpu.VMEM(lead + (6, 3, ROWS, w), BF16),
            pltpu.VMEM(lead + (4, ROWS, w), BF16),
            pltpu.VMEM(lead + (4, ROWS, w), BF16),
        ]

    shapes = (
        pltpu.VMEM((32, 512), F32),
        pltpu.VMEM((ROWS, 1024), F32),
        pltpu.VMEM((32, RANK), F32),
        pltpu.VMEM((4, RANK), F32),
    )
    grad_user, grad_feat, grad_item, grad_domain = pl.pallas_call(
        kernel,
        out_shape=shapes,
        in_specs=[pl.BlockSpec(memory_space=pltpu.HBM)] * 6,
        out_specs=[pl.BlockSpec(memory_space=pltpu.VMEM)] * 4,
        scratch_shapes=[
            pltpu.VMEM((512, 1024), BF16),
            pltpu.VMEM((4, 32, 512), BF16),
            pltpu.VMEM((512, 512), BF16),
            pltpu.VMEM((32, 512), BF16),
            pltpu.VMEM((4, 512), BF16),
            pltpu.VMEM((CHUNKS, 2, 6, 3, ROWS, width), BF16),
            pltpu.VMEM((512, 512), BF16),
            pltpu.VMEM((32, ROWS, 512), BF16),
            pltpu.VMEM((2, NZ, ROWS, 512), BF16),
            pltpu.VMEM((128, 512), BF16),
            pltpu.VMEM((128, 512), BF16),
            pltpu.VMEM((128, 512), F32),
            pltpu.VMEM((32, ROWS, 128), F32),
            pltpu.VMEM((32, ROWS, 512), F32),
            pltpu.VMEM((2, NZ, ROWS, 512), F32),
        ]
        + reduction((CHUNKS,), width)
        + reduction((), 128)
        + [
            pltpu.VMEM((ROWS, 128), F32),
            pltpu.VMEM((5, ROWS, 128), F32),
            pltpu.VMEM((ROWS, 128), F32),
            pltpu.VMEM((2, 6, 3, ROWS, 128), F32),
            pltpu.VMEM((32, ROWS, 512), F32),
            pltpu.VMEM((16, ROWS, 512), BF16),
            pltpu.VMEM((16, ROWS, 512), BF16),
            pltpu.VMEM((8, 32, 512), F32),
            pltpu.VMEM((8, 32, 512), BF16),
            pltpu.VMEM((3, 2, 32, 512), BF16),
            pltpu.VMEM((2, 32, 512), F32),
            pltpu.VMEM((32, 512), F32),
            pltpu.SemaphoreType.DMA((N_MESSAGES,)),
            pltpu.SemaphoreType.DMA((N_MESSAGES,)),
            pltpu.SemaphoreType.DMA((N_LOCAL,)),
        ],
        compiler_params=pltpu.CompilerParams(
            collective_id=0, has_side_effects=True, vmem_limit_bytes=63 << 20
        ),
        name="factor_gradients",
    )(side_matrix, slab, user_factor, feat_factor, item_factor, domain_factor)
    return grad_user.T, grad_feat, grad_item, grad_domain


def solution(mesh):
    return jax.shard_map(
        local,
        mesh=mesh,
        in_specs=(
            P("user", ("feat", "dom")),
            P("dom", "feat", "user"),
            P("user", None),
            P("user", ("feat", "dom")),
            P("feat", None),
            P("dom", None),
        ),
        out_specs=(
            P("user", ("feat", "dom")),
            P("user", ("feat", "dom")),
            P("feat", None),
            P("dom", None),
        ),
        check_vma=False,
    )
```

time: 72 us -> 68.9 us (0.957)
  local copies, waits for them, and re-layouts: 7.85 us -> 2.49 us
  Pallas kernels: 62.7 us -> 65.6 us
    unnamed x16 -> x4, local copies, waits for them, and re-layouts: 7.85 us -> 2.49 us
    pallas_call x1, Pallas kernels: 62.7 us -> 65.6 us  [local(): pl.pallas_call(kernel, out_shape=shapes, in_specs=[pl.BlockSpec(memory_sp...]
where the time goes in v2:
time: 68.9 us; the launch traced here: 68.8 us
  Pallas kernels  65.6 us (95%)
  local copies, waits for them, and re-layouts  2.49 us (4%)
    pallas_call x1, Pallas kernels, local(): pl.pallas_call(kernel, out_shape=shapes, in_specs=[pl.BlockSpec(memory_sp...  65.6 us
    unnamed x4, local copies, waits for them, and re-layouts  2.49 us

profile of v2, /device:TPU:24, one launch (start us, length us, event | category | flops | bytes accessed | tf_op | source)
XLA Modules:
  0.0 68.8 jit_solution(7680733372510828301)
XLA Ops:
  0.6 65.6 %factor_gradients.1 = (f32[32,512]{1,0:T(8,128)S(1)}, f32[16,1024]{1,0:T(8,128)S(1)}, f32[32,512]{1,0:T(8,128)S(1)}, f32[4,512]{1,0:T(4,128)S(1)}) custom-call(bf16[512,1024]{1,0:T(8,128)(2,1)} %side_h.1, bf16[4,32,512]{2,1,0:T(8,128)(2,1)} %slab_h.1, bf16[512,512]{1,0:T(8,128)(2,1)} %user_h.1, bf16[16,1024]{1,0:T(8,128)(2,1)} %feat_h.1, ...), custom_call_target="tpu_custom_call" | custom-call | tf_op jit(solution)/shard_map/factor_gradients/pallas_call | solution.py:357
  66.3 0.6 copy.14
  66.9 0.6 copy.17
  67.5 0.6 copy.15
  68.1 0.6 copy.16

commit v3 on v2

--- a/solution.py
+++ b/solution.py
@@ -42,8 +42,8 @@
     side, slab, user, items, domains,
     panel, user_rel, ut_abs, ut_rel,
     model_di, tensor_res, small, small_abs, tensor_user, side_user,
-    gf_other, gf_own, gf_x, gf_send, gf_near, gf_hub, gf_far,
-    sx_other, sx_own, sx_x, sx_send, sx_near, sx_hub, sx_far,
+    gf_own, gf_stage, gf_near, gf_other, gf_x, gf_hub, gf_far,
+    sx_own, sx_stage, sx_near, sx_other, sx_x, sx_hub, sx_far,
     row_send, row_recv, row_y, small_panel,
     su_all, su_core, su_core_recv, su_sum, su_send, su_recv, su_y, su_x,
     send_sems, recv_sems, local_sems,
@@ -94,16 +94,25 @@
         pl.semaphore_signal(barrier, inc=1, device_id=device, device_id_type=MESH)
     pl.semaphore_wait(barrier, len(greet))
 
+    def to_neighbours(g, state, plane, groups):
+        hub = g.at[plane, groups, 0]
+        state["near"].append(send(hub, g.at[plane, groups, 1], along(1)))
+        state["near"].append(send(hub, g.at[plane, groups, 2], along(-1)))
+
+    def to_far_end(g, state, plane):
+        state["near"].append(send(g.at[plane, 3, 0], g.at[plane, 5, 0], along(-2)))
+
     def gather_start(g):
         own = g.at[0, 0, 0]
         far = [send(own, g.at[0, h, 0], along(-HUBS[h])) for h in (1, 2)]
-        near = [send(own, g.at[0, 0, 1], along(1)), send(own, g.at[0, 0, 2], along(-1))]
-        return {"far": far, "near": near, "other": []}
+        other = send(own, g.at[1, 0, 0], along(0, 1))
+        state = {"far": far, "other": other, "near": []}
+        to_neighbours(g, state, 0, 0)
+        return state
 
     def gather_own(g, state):
-        for copy in state["near"]:
-            copy.wait_recv()
-        state["other"].append(send(g.at[0, 0], g.at[1, 0], along(0, 1)))
+        state["other"].wait_recv()
+        to_neighbours(g, state, 1, 0)
 
     def gather_hubs(g, state, lo):
         for copy in state["far"]:
@@ -113,60 +122,65 @@
                 send(g.at[0, h, 0], g.at[0, h + 2, 0], along(-HUBS[h])) for h in (1, 2)
             ]
         two = pl.ds(lo, 2)
-        hub = g.at[0, two, 0]
-        state["near"] = [send(hub, g.at[0, two, 1], along(1)), send(hub, g.at[0, two, 2], along(-1))]
+        state["other"] = send(g.at[0, two, 0], g.at[1, two, 0], along(0, 1))
+        to_neighbours(g, state, 0, two)
         if lo == 3:
-            state["near"].append(send(g.at[0, 3, 0], g.at[0, 5, 0], along(-2)))
-            state["other"].append(send(hub, g.at[1, two, 0], along(0, 1)))
-
-    def gather_near(g, state, lo):
+            to_far_end(g, state, 0)
+
+    def gather_other(g, state, lo):
+        state["other"].wait_recv()
+        to_neighbours(g, state, 1, pl.ds(lo, 2))
+        if lo == 3:
+            to_far_end(g, state, 1)
+
+    def gather_end(state):
         for copy in state["near"]:
             copy.wait_recv()
-        two = pl.ds(lo, 2)
-        if lo == 3:
-            rest = pl.ds(1, 2)
-            state["other"].append(send(g.at[0, two, rest], g.at[1, two, rest], along(0, 1)))
-            state["other"].append(send(g.at[0, 5, 0], g.at[1, 5, 0], along(0, 1)))
-        else:
-            state["other"].append(send(g.at[0, two], g.at[1, two], along(0, 1)))
-
-    def gather_end(state):
-        for copy in state["other"]:
-            copy.wait_recv()
-
-    groups = ((9, 16), (3, 9), (0, 3))
-
-    def reduce_start(other, x):
-        parts = [pl.ds(lo, hi - lo) for lo, hi in groups]
-        return {"x": [send(other.at[p], x.at[p], along(0, 1)) for p in parts], "near": {}, "far": []}
-
-    def reduce_near(own, x, stage, near, state, i):
-        lo, hi = groups[i]
-        state["x"][i].wait_recv()
-        total = own[lo:hi] + x[lo:hi].astype(F32)
-        own[lo:hi] = total
-        first, count = lo // 3, (hi - lo) // 3
-        for h in range(count):
-            stage[first + h] = total[3 * h : 3 * h + 3].astype(BF16)
-        some = pl.ds(first, count)
-        state["near"][i] = [
-            send(stage.at[some, 2], near.at[some, 2], along(1)),
-            send(stage.at[some, 1], near.at[some, 1], along(-1)),
-        ]
-        if i == 0:
-            stage[5, 0] = total[6].astype(BF16)
-            state["near"][i].append(send(stage.at[5, 0], near.at[5, 0], along(2)))
-
-    def reduce_far(own, near, hub, far, state, i):
+
+    groups = ((3, 2), (1, 2), (0, 1))
+
+    def reduce_split(slot_value, own, stage):
+        for plane in range(2):
+            for slot in range(NZ):
+                value, h, j = slot_value(plane, slot), slot // 3, slot % 3
+                if j == 0 and h < 5:
+                    own[plane, h] = value
+                else:
+                    stage[plane, h, j] = value.astype(BF16)
+
+    def reduce_start(stage, near):
+        state = {"near": [], "other": [], "far": []}
+        for first, count in groups:
+            some = pl.ds(first, count)
+            copies = [
+                send(stage.at[:, some, 2], near.at[:, some, 2], along(1)),
+                send(stage.at[:, some, 1], near.at[:, some, 1], along(-1)),
+            ]
+            if first == 3:
+                copies.append(send(stage.at[:, 5, 0], near.at[:, 5, 0], along(2)))
+            state["near"].append(copies)
+        return state
+
+    def reduce_hubs(own, near, other, x, state, i):
         for copy in state["near"][i]:
             copy.wait_recv()
-        lo, hi = groups[i]
-        for h in range(lo // 3, lo // 3 + (hi - lo) // 3):
-            total = own[3 * h] + near[h, 1].astype(F32) + near[h, 2].astype(F32)
+        first, count = groups[i]
+        for h in range(first, first + count):
+            total = own[:, h] + near[:, h, 1].astype(F32) + near[:, h, 2].astype(F32)
             if h == 3:
-                total = total + near[5, 0].astype(F32)
+                total = total + near[:, 5, 0].astype(F32)
+            own[0, h] = total[0]
+            other[h] = total[1].astype(BF16)
+        some = pl.ds(first, count)
+        state["other"].append(send(other.at[some], x.at[some], along(0, 1)))
+
+    def reduce_far(own, x, hub, far, state, i):
+        state["other"][i].wait_recv()
+        first, count = groups[i]
+        for h in range(first, first + count):
+            total = own[0, h] + x[h].astype(F32)
             if h == 0:
-                own[0] = total
+                own[0, 0] = total
             else:
                 hub[h - 1] = total.astype(BF16)
                 state["far"].append(send(hub.at[h - 1], far.at[h - 1], along(HUBS[h])))
@@ -174,7 +188,7 @@
     def reduce_end(own, far, state):
         for copy in state["far"]:
             copy.wait_recv()
-        total = own[0]
+        total = own[0, 0]
         for h in range(4):
             total = total + far[h].astype(F32)
         return total
@@ -209,10 +223,8 @@
         )
     small[0:32, :] = ITEM_SCALE * item_term
     small_abs[...] = small[...].T.reshape(32, ROWS, 128)
-    for slot in range(NZ):
-        sx_other[slot] = small_abs[absolute(1, slot)].astype(BF16)
-        sx_own[slot] = small_abs[absolute(0, slot)]
-    sx_state = reduce_start(sx_other, sx_x)
+    reduce_split(lambda plane, slot: small_abs[absolute(plane, slot)], sx_own, sx_stage)
+    sx_state = reduce_start(sx_stage, sx_near)
 
     ut_abs[...] = user[...].T.reshape(32, ROWS, 512)
     for plane in range(2):
@@ -223,23 +235,21 @@
         TENSOR_SCALE * dot(model_di[...], tensor_res[...], 0, 0)
     ).reshape(32, ROWS, 512)
 
-    for c in range(CHUNKS):
-        gather_own(panel.at[c], gathers[c])
+    def each(step, *more):
+        for c in range(CHUNKS):
+            step(panel.at[c], gathers[c], *more)
+
+    each(gather_own)
     for i in range(3):
-        reduce_near(sx_own, sx_x, sx_send, sx_near, sx_state, i)
-    for c in range(CHUNKS):
-        gather_hubs(panel.at[c], gathers[c], 1)
+        reduce_hubs(sx_own, sx_near, sx_other, sx_x, sx_state, i)
+    each(gather_hubs, 1)
     for i in range(3):
-        reduce_far(sx_own, sx_near, sx_hub, sx_far, sx_state, i)
-    for c in range(CHUNKS):
-        gather_near(panel.at[c], gathers[c], 1)
-    for c in range(CHUNKS):
-        gather_hubs(panel.at[c], gathers[c], 3)
-    for c in range(CHUNKS):
-        gather_near(panel.at[c], gathers[c], 3)
-
-    total = reduce_end(sx_own, sx_far, sx_state)
-    row_send[...] = total
+        reduce_far(sx_own, sx_x, sx_hub, sx_far, sx_state, i)
+    each(gather_other, 1)
+    each(gather_hubs, 3)
+    each(gather_other, 3)
+
+    row_send[...] = reduce_end(sx_own, sx_far, sx_state)
     row_copies = [send(row_send, row_recv.at[0], partner)]
     row_copies += [send(row_send, row_recv.at[dy], beside(dy)) for dy in range(1, 4)]
 
@@ -251,21 +261,20 @@
         blocks = [panel[c, p].reshape(18 * ROWS, width)[0:256] for p in range(2)]
         model = dot(user_rel[:, 0:256], blocks[0]) + dot(user_rel[:, 256:512], blocks[1])
         res = (model - side[:, c * width : (c + 1) * width].astype(F32)).astype(BF16)
-        gf_other[c] = dot(ut_rel[1].reshape(256, 512), res).reshape(NZ, ROWS, width).astype(BF16)
-        gf_state.append(reduce_start(gf_other.at[c], gf_x.at[c]))
-        gf_own[c] = dot(ut_rel[0].reshape(256, 512), res).reshape(NZ, ROWS, width)
+        part = dot(ut_rel[...].reshape(512, 512), res).reshape(2, NZ, ROWS, width)
+        reduce_split(lambda plane, slot: part[plane, slot], gf_own.at[c], gf_stage.at[c])
+        gf_state.append(reduce_start(gf_stage.at[c], gf_near.at[c]))
         for p in range(2):
-            part = dot(blocks[p], res, 1, 1).reshape(NZ, ROWS, 512)
-            side_user[p] = part if c == 0 else side_user[p] + part
+            user_part = dot(blocks[p], res, 1, 1).reshape(NZ, ROWS, 512)
+            side_user[p] = user_part if c == 0 else side_user[p] + user_part
 
     compute(0)
-    compute(1)
-
     for copy in row_copies:
         copy.wait_recv()
     lane = lax.broadcasted_iota(jnp.int32, (ROWS, 128), 1)
     row_y[...] = row_send[...] + row_recv[1] + row_recv[2] + row_recv[3]
     row_copy = send(row_y, row_recv.at[4], opposite)
+    compute(1)
 
     for plane in range(2):
         for slot in range(NZ):
@@ -275,13 +284,21 @@
     su_core[...] = su_all[16:].astype(BF16)
     su_copy = send(su_core, su_core_recv, partner)
 
-    def gf_near_step(c, i):
-        reduce_near(gf_own.at[c], gf_x.at[c], gf_send.at[c], gf_near.at[c], gf_state[c], i)
-
-    def gf_far_step(c, i):
-        reduce_far(gf_own.at[c], gf_near.at[c], gf_hub.at[c], gf_far.at[c], gf_state[c], i)
-
-    gf_near_step(0, 0)
+    def hubs_step(c, i):
+        reduce_hubs(gf_own.at[c], gf_near.at[c], gf_other.at[c], gf_x.at[c], gf_state[c], i)
+
+    def far_step(c, i):
+        reduce_far(gf_own.at[c], gf_x.at[c], gf_hub.at[c], gf_far.at[c], gf_state[c], i)
+
+    hubs_step(0, 0)
+    row_copy.wait_recv()
+    small_panel[0, 0, 0] = jnp.where(
+        lane < 32, row_send[...] + row_recv[0], row_y[...] + row_recv[4]
+    )
+    small_gather = gather_start(small_panel)
+    hubs_step(0, 1)
+    hubs_step(0, 2)
+    hubs_step(1, 0)
     su_copy.wait_recv()
     su_sum[...] = (su_all[:16] + su_core_recv[...].astype(F32)).reshape(8, 32, 512)
     su_send[...] = su_sum[...].astype(BF16)
@@ -289,18 +306,16 @@
         send(su_send.at[pl.ds((y + dy) % 4 * 2, 2)], su_recv.at[dy - 1], beside(dy))
         for dy in range(1, 4)
     ]
-    gf_near_step(0, 1)
-    row_copy.wait_recv()
-    small_panel[0, 0, 0] = jnp.where(
-        lane < 32, row_send[...] + row_recv[0], row_y[...] + row_recv[4]
-    )
-    small_gather = gather_start(small_panel)
-    gf_near_step(0, 2)
-    gf_far_step(0, 0)
-    gf_near_step(1, 0)
+    hubs_step(1, 1)
+    hubs_step(1, 2)
+    far_step(0, 0)
     gather_own(small_panel, small_gather)
-    gf_far_step(0, 1)
-    gf_near_step(1, 1)
+    far_step(0, 1)
+    far_step(0, 2)
+    far_step(1, 0)
+    gather_hubs(small_panel, small_gather, 1)
+    far_step(1, 1)
+    far_step(1, 2)
     for copy in su_copies:
         copy.wait_recv()
     for i in range(2):
@@ -309,20 +324,15 @@
             grad = grad + su_recv[dy, i].astype(F32)
         su_y[i] = grad
     su_copy = send(su_y.at[1 - xh], su_x, opposite)
-    gf_far_step(1, 0)
-    gf_near_step(1, 2)
-    gather_hubs(small_panel, small_gather, 1)
-    gf_far_step(1, 1)
-    gf_far_step(0, 2)
-    gf_far_step(1, 2)
-    gather_near(small_panel, small_gather, 1)
+    gather_other(small_panel, small_gather, 1)
     gather_hubs(small_panel, small_gather, 3)
-    gather_near(small_panel, small_gather, 3)
-
     su_copy.wait_recv()
     gu_ref[...] = su_y[xh] + su_x[...]
-    gf_ref[:, 0:width] = FEAT_SCALE * reduce_end(gf_own.at[0], gf_far.at[0], gf_state[0])
-    gf_ref[:, width:] = FEAT_SCALE * reduce_end(gf_own.at[1], gf_far.at[1], gf_state[1])
+    gather_other(small_panel, small_gather, 3)
+    for c in range(CHUNKS):
+        gf_ref[:, c * width : (c + 1) * width] = FEAT_SCALE * reduce_end(
+            gf_own.at[c], gf_far.at[c], gf_state[c]
+        )
     gather_end(small_gather)
     for plane in range(2):
         for slot in range(NZ):
@@ -339,11 +349,11 @@
 
     def reduction(lead, w):
         return [
-            pltpu.VMEM(lead + (NZ, ROWS, w), BF16),
-            pltpu.VMEM(lead + (NZ, ROWS, w), F32),
-            pltpu.VMEM(lead + (NZ, ROWS, w), BF16),
-            pltpu.VMEM(lead + (6, 3, ROWS, w), BF16),
-            pltpu.VMEM(lead + (6, 3, ROWS, w), BF16),
+            pltpu.VMEM(lead + (2, 5, ROWS, w), F32),
+            pltpu.VMEM(lead + (2, 6, 3, ROWS, w), BF16),
+            pltpu.VMEM(lead + (2, 6, 3, ROWS, w), BF16),
+            pltpu.VMEM(lead + (5, ROWS, w), BF16),
+            pltpu.VMEM(lead + (5, ROWS, w), BF16),
             pltpu.VMEM(lead + (4, ROWS, w), BF16),
             pltpu.VMEM(lead + (4, ROWS, w), BF16),
         ]

time: 68.9 us -> 64 us (0.929); the launches traced: 68.8 us -> 63.1 us
  Pallas kernels: 65.6 us -> 60 us
    pallas_call x1, Pallas kernels: 65.6 us -> 60 us  [local(): pl.pallas_call(kernel, out_shape=shapes, in_specs=[pl.BlockSpec(memory_sp...]
where the time goes in v3:
time: 64 us; the launch traced here: 63.1 us
  Pallas kernels  60 us (94%)
  local copies, waits for them, and re-layouts  2.49 us (4%)
  between operations  0.64 us (1%)
    pallas_call x1, Pallas kernels, local(): pl.pallas_call(kernel, out_shape=shapes, in_specs=[pl.BlockSpec(memory_sp...  60 us
    unnamed x4, local copies, waits for them, and re-layouts  2.49 us

profile of v3, /device:TPU:24, one launch (start us, length us, event | category | flops | bytes accessed | tf_op | source)
XLA Modules:
  0.0 63.1 jit_solution(10392045443164143724)
XLA Ops:
  0.6 60.0 %factor_gradients.1 = (f32[32,512]{1,0:T(8,128)S(1)}, f32[16,1024]{1,0:T(8,128)S(1)}, f32[32,512]{1,0:T(8,128)S(1)}, f32[4,512]{1,0:T(4,128)S(1)}) custom-call(bf16[512,1024]{1,0:T(8,128)(2,1)} %side_h.1, bf16[4,32,512]{2,1,0:T(8,128)(2,1)} %slab_h.1, bf16[512,512]{1,0:T(8,128)(2,1)} %user_h.1, bf16[16,1024]{1,0:T(8,128)(2,1)} %feat_h.1, ...), custom_call_target="tpu_custom_call" | custom-call | tf_op jit(solution)/shard_map/factor_gradients/pallas_call | solution.py:367
  60.6 0.6 %copy.14 = f32[512,32]{0,1:T(8,128)} copy(f32[512,32]{0,1:T(8,128)S(1)} %bitcast.1) | data formatting | bytes 131072
  61.2 0.6 copy.17
  61.8 0.6 copy.15
  62.5 0.6 copy.16

commit v4 on v3

--- a/solution.py
+++ b/solution.py
@@ -247,12 +247,11 @@
         reduce_far(sx_own, sx_x, sx_hub, sx_far, sx_state, i)
     each(gather_other, 1)
     each(gather_hubs, 3)
-    each(gather_other, 3)
-
     row_send[...] = reduce_end(sx_own, sx_far, sx_state)
     row_copies = [send(row_send, row_recv.at[0], partner)]
     row_copies += [send(row_send, row_recv.at[dy], beside(dy)) for dy in range(1, 4)]
 
+    each(gather_other, 3)
     side_copy.wait()
     gf_state = []
 
@@ -268,13 +267,24 @@
             user_part = dot(blocks[p], res, 1, 1).reshape(NZ, ROWS, 512)
             side_user[p] = user_part if c == 0 else side_user[p] + user_part
 
-    compute(0)
     for copy in row_copies:
         copy.wait_recv()
     lane = lax.broadcasted_iota(jnp.int32, (ROWS, 128), 1)
     row_y[...] = row_send[...] + row_recv[1] + row_recv[2] + row_recv[3]
     row_copy = send(row_y, row_recv.at[4], opposite)
+
+    compute(0)
     compute(1)
+
+    row_copy.wait_recv()
+    mine = jnp.where(lane < 32, row_send[...] + row_recv[0], row_y[...] + row_recv[4])
+    small_panel[0, 0] = jnp.concatenate([mine[0:8, 0:64], mine[8:16, 0:64]], axis=1)
+    small_copies = [
+        send(small_panel.at[0, 0], small_panel.at[plane, slot], along(-SLOTS[slot], plane))
+        for slot in range(NZ - 1, -1, -1)
+        for plane in range(2)
+        if slot + plane > 0
+    ]
 
     for plane in range(2):
         for slot in range(NZ):
@@ -290,14 +300,8 @@
     def far_step(c, i):
         reduce_far(gf_own.at[c], gf_x.at[c], gf_hub.at[c], gf_far.at[c], gf_state[c], i)
 
-    hubs_step(0, 0)
-    row_copy.wait_recv()
-    small_panel[0, 0, 0] = jnp.where(
-        lane < 32, row_send[...] + row_recv[0], row_y[...] + row_recv[4]
-    )
-    small_gather = gather_start(small_panel)
-    hubs_step(0, 1)
-    hubs_step(0, 2)
+    for i in range(3):
+        hubs_step(0, i)
     hubs_step(1, 0)
     su_copy.wait_recv()
     su_sum[...] = (su_all[:16] + su_core_recv[...].astype(F32)).reshape(8, 32, 512)
@@ -308,12 +312,9 @@
     ]
     hubs_step(1, 1)
     hubs_step(1, 2)
-    far_step(0, 0)
-    gather_own(small_panel, small_gather)
-    far_step(0, 1)
-    far_step(0, 2)
+    for i in range(3):
+        far_step(0, i)
     far_step(1, 0)
-    gather_hubs(small_panel, small_gather, 1)
     far_step(1, 1)
     far_step(1, 2)
     for copy in su_copies:
@@ -324,19 +325,19 @@
             grad = grad + su_recv[dy, i].astype(F32)
         su_y[i] = grad
     su_copy = send(su_y.at[1 - xh], su_x, opposite)
-    gather_other(small_panel, small_gather, 1)
-    gather_hubs(small_panel, small_gather, 3)
     su_copy.wait_recv()
     gu_ref[...] = su_y[xh] + su_x[...]
-    gather_other(small_panel, small_gather, 3)
     for c in range(CHUNKS):
         gf_ref[:, c * width : (c + 1) * width] = FEAT_SCALE * reduce_end(
             gf_own.at[c], gf_far.at[c], gf_state[c]
         )
-    gather_end(small_gather)
+    for copy in small_copies:
+        copy.wait_recv()
     for plane in range(2):
         for slot in range(NZ):
-            small_abs[absolute(plane, slot)] = small_panel[plane, slot // 3, slot % 3]
+            b, both = absolute(plane, slot), small_panel[plane, slot]
+            small_abs[b, 0:8] = both
+            small_abs[b, 8:16] = jnp.concatenate([both[:, 64:], both[:, :64]], axis=1)
     small[...] = small_abs[...].reshape(512, 128).T
     gi_ref[...] = small[0:32, :]
     gd_ref[...] = small[32:36, :]
@@ -392,7 +393,7 @@
             pltpu.VMEM((ROWS, 128), F32),
             pltpu.VMEM((5, ROWS, 128), F32),
             pltpu.VMEM((ROWS, 128), F32),
-            pltpu.VMEM((2, 6, 3, ROWS, 128), F32),
+            pltpu.VMEM((2, NZ, 8, 128), F32),
             pltpu.VMEM((32, ROWS, 512), F32),
             pltpu.VMEM((16, ROWS, 512), BF16),
             pltpu.VMEM((16, ROWS, 512), BF16),

time: 64 us -> 63 us (0.984)
  the two profiles are of different devices: /device:TPU:24 before, /device:TPU:2 now
where the time goes in v4:
time: 63 us; the launch traced here: 62.9 us
  Pallas kernels  59.7 us (95%)
  local copies, waits for them, and re-layouts  2.49 us (4%)
  between operations  0.64 us (1%)
    pallas_call x1, Pallas kernels, local(): pl.pallas_call(kernel, out_shape=shapes, in_specs=[pl.BlockSpec(memory_sp...  59.7 us
    unnamed x4, local copies, waits for them, and re-layouts  2.49 us

profile of v4, /device:TPU:2, one launch (start us, length us, event | category | flops | bytes accessed | tf_op | source)
XLA Modules:
  0.0 62.9 jit_solution(2499669831674515742)
XLA Ops:
  0.6 59.7 %factor_gradients.1 = (f32[32,512]{1,0:T(8,128)S(1)}, f32[16,1024]{1,0:T(8,128)S(1)}, f32[32,512]{1,0:T(8,128)S(1)}, f32[4,512]{1,0:T(4,128)S(1)}) custom-call(bf16[512,1024]{1,0:T(8,128)(2,1)} %side_h.1, bf16[4,32,512]{2,1,0:T(8,128)(2,1)} %slab_h.1, bf16[512,512]{1,0:T(8,128)(2,1)} %user_h.1, bf16[16,1024]{1,0:T(8,128)(2,1)} %feat_h.1, ...), custom_call_target="tpu_custom_call" | custom-call | tf_op jit(solution)/shard_map/factor_gradients/pallas_call | solution.py:368
  60.4 0.6 %copy.14 = f32[512,32]{0,1:T(8,128)} copy(f32[512,32]{0,1:T(8,128)S(1)} %bitcast.1) | data formatting | bytes 131072
  61.0 0.6 copy.17
  61.6 0.6 %copy.15 = f32[16,1024]{1,0:T(8,128)} copy(f32[16,1024]{1,0:T(8,128)S(1)} %get-tuple-element.13) | data formatting | bytes 131072
  62.2 0.6 %copy.16 = f32[32,512]{1,0:T(8,128)} copy(f32[32,512]{1,0:T(8,128)S(1)} %get-tuple-element.14) | data formatting | bytes 131072
